TPU v7x, 512 devices: a whole 4x4x16 slice. The times are simulated.
512 devices in a mesh: dp: 32 (over z, y_lo), mp: 16 (over y_hi, x, core).
Axes of the slice: x: 4, y: 4 (y_hi: 2, y_lo: 2; y = y_hi * 2 + y_lo), z: 16, core: 2. Of those that a mesh axis runs over, the one named last changes fastest.
Arguments:
- grads: bfloat16 [32, 32, 512, 512], P('dp', 'mp'), may hold values from -3500 to 3500
- order: int32 [16, 4], P('mp'), may hold values from 0 to 3, each once within a row
- offset: int32 [16], P('mp'), may hold values from 0 to 3
- prev_roots: bfloat16 [64, 512, 512], P('mp'), may hold values from -0.1 to 1.5
Outputs:
- update: bfloat16 [32, 32, 512, 512], P('dp', 'mp')
Inputs may be any that keep to these rules, and one draw needn't show every extreme that they name: `order`: each row holds every number of 0 to 3 once.
All inputs are finite; a program needn't handle non-finite values.
Results may differ from a plain program's by a relative error of at most 0.0019.
The roundings to bfloat16 on the way count: a program that leaves them out, or rounds other values in their place, can miss the bound.
Values may be sent and summed in bfloat16 or wider, within the bound.
A program may use at most 64 MiB of HBM per device.

v0:
```python
import jax
import jax.numpy as jnp
from jax import lax
from jax.sharding import PartitionSpec as P

REFRESH = 2
ITERS = 3


ridge = 0.1


def from_root(block, axis, source):
    block = jnp.where(lax.axis_index(axis) == source, block, jnp.zeros_like(block))
    return lax.psum(block, axis)


def product(first, second):
    return jnp.dot(first, second, precision=lax.Precision.HIGHEST)


def full_newton(statistic, scale_div):
    block_size = statistic.shape[0]
    identity = jnp.eye(block_size, dtype=jnp.float32)
    ridged = statistic / scale_div + ridge * identity
    start_scale = 2.5 / jnp.sqrt(jnp.sum(ridged * ridged))
    current = start_scale * ridged
    root_now = jnp.sqrt(jnp.sqrt(start_scale)) * identity
    for step_index in range(ITERS):
        factor = (5.0 * identity - current) * 0.25
        root_now = product(root_now, factor)
        if step_index < ITERS - 1:
            factor_sq = product(factor, factor)
            current = product(product(factor_sq, factor_sq), current)
    return root_now.astype(jnp.bfloat16)


def body(grads, order, offset, prev_roots):
    own_grads = grads[0]
    block_size = own_grads.shape[1]
    item_count = order.shape[1]
    replicas = lax.axis_size("dp")
    scale_div = float(block_size * replicas)
    slot_list = (offset[0] + jnp.arange(REFRESH, dtype=jnp.int32)) % item_count
    chosen = order[0][slot_list]

    def local_stat(item_index):
        picked = own_grads[item_index // 2]
        turned = jnp.where(item_index % 2 == 0, picked, picked.T)
        return lax.dot_general(
            turned, turned, (((1,), (1,)), ((), ())), preferred_element_type=jnp.float32
        )

    statistics = jax.vmap(local_stat)(chosen)
    summed = lax.psum(statistics, "dp")
    position = lax.axis_index("dp")
    mine = summed[jnp.minimum(position, REFRESH - 1)]
    own_root = lax.cond(
        position < REFRESH,
        lambda operand: full_newton(operand, scale_div),
        lambda operand: jnp.zeros((block_size, block_size), jnp.bfloat16),
        mine,
    )
    received = [from_root(own_root, "dp", slot_number) for slot_number in range(REFRESH)]
    fresh = jnp.stack(received)
    roots = prev_roots.at[chosen].set(fresh)
    left_roots = roots[0::2]
    right_roots = roots[1::2]
    half_done = jnp.einsum(
        "bij,bjk->bik", left_roots, own_grads, preferred_element_type=jnp.float32
    ).astype(jnp.bfloat16)
    unscaled = jnp.einsum(
        "bij,bjk->bik", half_done, right_roots, preferred_element_type=jnp.float32
    )
    grad_float = own_grads.astype(jnp.float32)
    grad_sq = jnp.sum(grad_float * grad_float)
    pre_sq = jnp.sum(unscaled * unscaled)
    grad_total, pre_total = lax.psum((grad_sq, pre_sq), "mp")
    scaled = unscaled * jnp.sqrt(grad_total / (pre_total + 1e-06))
    return scaled.astype(jnp.bfloat16)[None]


def solution(mesh):
    placed = (P("dp", "mp", None, None), P("mp", None), P("mp"), P("mp", None, None))
    return jax.shard_map(
        body, mesh=mesh, in_specs=placed, out_specs=P("dp", "mp", None, None), check_vma=False
    )
```

profile of v0, /device:TPU:1, one launch (start us, length us, event | category | flops | bytes accessed | tf_op | source)
XLA Modules:
  0.0 619.7 jit_solution(3931548302331572488)
XLA Ops:
  6.5 0.0 copy-start
  6.5 0.0 copy-start.2
  6.5 0.0 all-reduce.6.cloned.1.call-start
  7.3 0.0 copy-done
  7.3 0.6 gather_fusion
  8.0 0.0 copy-done.2
  8.0 0.6 gather_fusion.1
  8.6 0.5 copy.8
  9.2 2.1 fusion.63
  11.3 0.0 all-reduce.6.cloned.1.call-update
  11.3 0.0 all-reduce.8.cloned.1.call-start
  11.4 254.9 %all-reduce.6.cloned.1.call-done = f32[2,512,512]{2,1,0:T(8,128)} async-done(((f32[2,512,512]{2,1,0:T(8,128)}), f32[2,512,512]{2,1,0:T(8,128)}) %all-reduce.6.cloned.1.call-update) | async-done | bytes 2097168 | tf_op jit(solution)/shard_map/psum | solution.py:55
  266.3 23.3 %conditional.1 = (bf16[512,512]{1,0:T(8,128)(2,1)S(1)}) conditional(s32[]{:T(128)} %convert_element_type.18, () %tuple.17, (s32[]{:T(128)}, f32[2,512,512]{2,1,0:T(8,128)}) %tuple.18), branch_computations={%region_1.2_spmd, %region_2.4_spmd} | conditional | flops 14506524672 | bytes 31981722 | solution.py:58
  266.3 2.1 multiply_reduce_fusion
  269.1 3.7 fusion.5
  272.8 0.0 copy-start.3
  272.8 1.8 fusion.82
  274.6 0.0 copy-done.3
  274.6 1.9 fusion.14
  276.6 1.9 fusion.17
  278.5 1.8 fusion.83
  280.3 1.9 fusion
  282.3 3.3 fusion.2
  285.6 1.9 fusion.19
  287.5 1.9 convolution_convert_fusion
  289.6 1.1 select_bitcast_fusion.1
  290.7 0.0 copy-start.1
  290.7 0.0 all-reduce.8.cloned.1.call-update
  290.7 1.1 multiply_reduce_fusion.2
  291.8 256.2 %all-reduce.8.cloned.1.call-done = (bf16[1,512,512]{2,1,0:T(8,128)(2,1)}, bf16[1,512,512]{2,1,0:T(8,128)(2,1)}) async-done(((bf16[1,512,512]{2,1,0:T(8,128)(2,1)}, bf16[1,512,512]{2,1,0:T(8,128)(2,1)}), (bf16[1,512,512]{2,1,0:T(8,128)(2,1)}, bf16[1,512,512]{2,1,0:T(8,128)(2,1)})) %all-reduce.8.cloned.1.call-update) | async-done | bytes 1048592 | tf_op jit(solution)/shard_map/psum | solution.py:15
  548.1 1.3 pad_maximum_fusion
  549.4 0.0 copy-done.1
  549.4 0.8 scatter_fusion
  550.2 4.4 multiply_reduce_fusion.1
  554.6 54.0 %all-reduce.1 = (f32[]{:T(128)}, f32[]{:T(128)}) all-reduce(f32[]{:T(128)} %multiply_reduce_fusion.2, f32[]{:T(128)} %get-tuple-element.57), channel_id=1, replica_groups=mesh['dp'=32,'mp'=16] {'mp'}, use_global_device_ids=true, to_apply=%region_8.9 | all-reduce | flops 2 | bytes 16 | tf_op jit(solution)/shard_map/psum | solution.py:78
  610.0 2.8 fusion.62
  (4 shorter events, 0.0 us)
Async XLA Ops:
  6.5 0.8 copy-start
  6.5 1.5 copy-start.2
  6.5 259.8 %all-reduce.6.cloned.1.call-start = ((), (), s32[]{:S(2)}) async-start(), calls=%async_computation | async-start | bytes 4194304 | tf_op jit(solution)/shard_map/psum | solution.py:55
  11.3 536.7 %all-reduce.8.cloned.1.call-start = ((), (), s32[]{:S(2)}) async-start(), calls=%async_computation.1 | async-start | bytes 2097152 | tf_op jit(solution)/shard_map/psum | solution.py:15
  272.8 1.9 copy-start.3
  290.7 258.7 %copy-start.1 = (bf16[4,512,512]{2,1,0:T(8,128)(2,1)S(1)}, bf16[4,512,512]{2,1,0:T(8,128)(2,1)}, u32[]{:S(2)}) copy-start(bf16[4,512,512]{2,1,0:T(8,128)(2,1)} %param.9) | copy-start | bytes 6291460
Sparse Core Ops, SparseCore 0:
  11.5 254.7 all-reduce.5
  290.8 257.2 all-reduce.7
where the time goes:
time: 620 us
  waiting for transfers between devices  511 us (82%)
  blocking collectives  54 us (9%)
  matrix products  26.7 us (4%)
  between operations  15.5 us (2%)
  other arithmetic  8.49 us (1%)
    psum x1, waiting for transfers between devices, from_root(): return lax.psum(block, axis)  256 us
    psum x1, waiting for transfers between devices, body(): summed = lax.psum(statistics, 'dp')  255 us
    psum x1, blocking collectives, body(): grad_total, pre_total = lax.psum((grad_sq, pre_sq), 'mp')  54 us
    dot_general x9, matrix products, product(): return jnp.dot(first, second, precision=lax.Precision.HIGHEST)  20.1 us
  transfers between devices with their start and end apart: 2, of which 2 were waited for; matrix products, arithmetic and copies ran while one was open for 0% of the time, Pallas kernels for 0%

commit v1 on v0

v1 whole, which is shorter than its diff:
```python
import functools

import jax
import jax.numpy as jnp
from jax import lax
from jax.experimental import pallas as pl
from jax.experimental.pallas import tpu as pltpu
from jax.sharding import PartitionSpec as P

MESH = pl.DeviceIdType.MESH
N = 512
T = 128
REPLICAS = 32
RING = 16
PEERS = 16
RIDGE = 0.1
PAIRS = [(i, j) for i in range(N // T) for j in range(i, N // T)]
ROWS = len(PAIRS) * T
PARTS = 2
PART = ROWS // PARTS
MEMBERS = (1, 2, -1)
LEADERS = (4, -4, 8)


def part(index):
    return pl.ds(index * PART, PART)


def small(a, b):
    return jnp.dot(a.astype(jnp.bfloat16), b.astype(jnp.bfloat16), preferred_element_type=jnp.float32)


def upper(full):
    return [full[i * T:(i + 1) * T, j * T:(j + 1) * T] for i, j in PAIRS]


def unpack(packed_ref, full_ref, scale=None):
    for index, (i, j) in enumerate(PAIRS):
        block = packed_ref[index * T:(index + 1) * T, :]
        full_ref[i * T:(i + 1) * T, j * T:(j + 1) * T] = block
        if i != j:
            full_ref[j * T:(j + 1) * T, i * T:(i + 1) * T] = block.T


def next_state(a):
    e2 = (small(a, a) - 10.0 * a) * 0.0625
    e4 = 3.125 * e2 + small(e2, e2)
    return 2.44140625 * a + small(e4, a)


def inverse_root(stat):
    row = lax.broadcasted_iota(jnp.int32, (N, N), 0)
    column = lax.broadcasted_iota(jnp.int32, (N, N), 1)
    eye = jnp.where(row == column, 1.0, 0.0)
    ridged = stat * (1.0 / (N * REPLICAS)) + RIDGE * eye
    total = jnp.sum(jnp.sum(ridged * ridged, axis=0, keepdims=True), axis=1, keepdims=True)
    start = 2.5 / jnp.sqrt(total)
    a = start * ridged
    b = next_state(a)
    c = next_state(b)
    g = small(a, b) * 0.0625 - 0.3125 * (a + b)
    root = 1.953125 * eye + 1.25 * g - 0.390625 * c - 0.25 * small(g, c)
    return jnp.sqrt(jnp.sqrt(start)) * root


def kernel(order, offset, grads, prev, out, old, stat, mine, sent, near, far, across, fresh, full, work, half, norms,
           old_sem, near_send, near_recv, far_send, far_recv, across_send, across_recv, fresh_send, fresh_recv,
           norm_send, norm_recv):
    dp, mp = lax.axis_index("dp"), lax.axis_index("mp")
    z, core = dp // 2, mp % 2
    sign = 1 - 2 * core

    def along(step):
        return (lax.rem(dp + 2 * step + 2 * RING, 2 * RING), mp)

    beside = (dp + 1 - 2 * (dp % 2), mp)

    load_old = pltpu.make_async_copy(prev, old, old_sem)
    load_old.start()

    barrier = pltpu.get_barrier_semaphore()
    for step in (1, -1, 2, -2, 4, -4, 8):
        pl.semaphore_signal(barrier, inc=1, device_id=along(step), device_id_type=MESH)
    pl.semaphore_signal(barrier, inc=1, device_id=beside, device_id_type=MESH)

    def greet(k, unused):
        pl.semaphore_signal(barrier, inc=1, device_id=(dp, lax.rem(mp + k, PEERS)), device_id_type=MESH)
        return unused

    lax.fori_loop(1, PEERS, greet, 0)

    place = [lax.rem(sign * (z - 5 * (2 * slot + core)) + 8 * RING, RING) for slot in range(2)]
    role = [lax.rem(p, 4) for p in place]
    leads = jnp.logical_or(role[0] == 0, role[1] == 0)
    lead_slot = jnp.where(role[1] == 0, 1, 0)
    lead_place = jnp.where(role[1] == 0, place[1], place[0])
    is_root = jnp.logical_and(leads, lead_place == 0)
    is_leaf_leader = jnp.logical_and(leads, lead_place != 0)

    items = [order[0, (offset[0] + slot) % 4] for slot in range(2)]

    def send_near(slot, k, index):
        return pltpu.make_async_remote_copy(
            src_ref=sent.at[slot, part(index)], dst_ref=near.at[k, part(index)],
            send_sem=near_send.at[slot, index], recv_sem=near_recv.at[k, index],
            device_id=along(-sign * MEMBERS[k]), device_id_type=MESH)

    for slot in range(2):
        item = items[slot]
        picked = grads[0, item // 2]
        turned = jnp.where(item % 2 == 0, picked, picked.T)
        product = lax.dot_general(turned, turned, (((1,), (1,)), ((), ())), preferred_element_type=jnp.float32)
        for index, block in enumerate(upper(product)):
            stat[slot, index * T:(index + 1) * T, :] = block
            sent[slot, index * T:(index + 1) * T, :] = block.astype(jnp.bfloat16)
        if slot == 0:
            pl.semaphore_wait(barrier, 7 + 1 + PEERS - 1)
        for k in range(3):
            @pl.when(role[slot] == k + 1)
            def _():
                for index in range(PARTS):
                    send_near(slot, k, index).start()

    grad_sq = jnp.zeros((1, 1), jnp.float32)
    for b in range(2):
        value = grads[0, b].astype(jnp.float32)
        grad_sq += jnp.sum(jnp.sum(value * value, axis=0, keepdims=True), axis=1, keepdims=True)

    def send_far(k, index):
        return pltpu.make_async_remote_copy(
            src_ref=mine.at[part(index)], dst_ref=far.at[k, part(index)],
            send_sem=far_send.at[index], recv_sem=far_recv.at[k, index],
            device_id=along(-sign * LEADERS[k]), device_id_type=MESH)

    def send_across(index):
        return pltpu.make_async_remote_copy(
            src_ref=mine.at[part(index)], dst_ref=across.at[part(index)],
            send_sem=across_send.at[index], recv_sem=across_recv.at[index],
            device_id=beside, device_id_type=MESH)

    @pl.when(leads)
    def _():
        for index in range(PARTS):
            for k in range(3):
                send_near(0, k, index).wait_recv()
            total = stat[lead_slot, part(index)]
            for k in range(3):
                total += near[k, part(index)].astype(jnp.float32)
            work[part(index)] = total
            mine[part(index)] = total.astype(jnp.bfloat16)
            for k in range(3):
                @pl.when(lead_place == LEADERS[k] % RING)
                def _():
                    send_far(k, index).start()

    def send_fresh(slot, step, k, index):
        return pltpu.make_async_remote_copy(
            src_ref=fresh.at[slot, part(index)], dst_ref=fresh.at[slot, part(index)],
            send_sem=fresh_send.at[k, index], recv_sem=fresh_recv.at[slot, index],
            device_id=along(step), device_id_type=MESH)

    @pl.when(is_root)
    def _():
        for index in range(PARTS):
            for k in range(3):
                send_far(k, index).wait_recv()
            total = work[part(index)]
            for k in range(3):
                total += far[k, part(index)].astype(jnp.float32)
            work[part(index)] = total
            mine[part(index)] = total.astype(jnp.bfloat16)
            send_across(index).start()
        for index in range(PARTS):
            send_across(index).wait_recv()
            work[part(index)] += across[part(index)].astype(jnp.float32)
        unpack(work, full)
        root = inverse_root(full[...])
        for index, block in enumerate(upper(root)):
            fresh[lead_slot, index * T:(index + 1) * T, :] = block.astype(jnp.bfloat16)
        for index in range(PARTS):
            for k, step in enumerate(LEADERS + MEMBERS):
                send_fresh(lead_slot, sign * step, k, index).start()

    @pl.when(is_leaf_leader)
    def _():
        for index in range(PARTS):
            send_fresh(lead_slot, 1, 0, index).wait_recv()
            for k, step in enumerate(MEMBERS):
                send_fresh(lead_slot, sign * step, 3 + k, index).start()

    load_old.wait()
    for slot in range(2):
        @pl.when(role[slot] != 0)
        def _():
            for index in range(PARTS):
                send_fresh(slot, 1, 0, index).wait_recv()
        unpack(fresh.at[slot], half.at[slot])

    pre_sq = jnp.zeros((1, 1), jnp.float32)
    for b in range(2):
        pair = []
        for side in range(2):
            k = 2 * b + side
            pair.append(jnp.where(items[0] == k, half[0], jnp.where(items[1] == k, half[1], old[k])))
        done = jnp.dot(pair[0], grads[0, b], preferred_element_type=jnp.float32).astype(jnp.bfloat16)
        unscaled = jnp.dot(done, pair[1], preferred_element_type=jnp.float32)
        full2 = unscaled
        pre_sq += jnp.sum(jnp.sum(full2 * full2, axis=0, keepdims=True), axis=1, keepdims=True)
        if b == 0:
            full[...] = unscaled
        else:
            last = unscaled

    line = lax.broadcasted_iota(jnp.int32, (8, T), 0)
    norms[mp] = jnp.where(line == 0, grad_sq, pre_sq)

    def send_norm(k):
        return pltpu.make_async_remote_copy(
            src_ref=norms.at[mp], dst_ref=norms.at[mp], send_sem=norm_send.at[k], recv_sem=norm_recv.at[mp],
            device_id=(dp, lax.rem(mp + k, PEERS)), device_id_type=MESH)

    def recv_norm(k):
        source = lax.rem(mp + k, PEERS)
        return pltpu.make_async_remote_copy(
            src_ref=norms.at[source], dst_ref=norms.at[source], send_sem=norm_send.at[k], recv_sem=norm_recv.at[source],
            device_id=(dp, source), device_id_type=MESH)

    def start_norm(k, unused):
        send_norm(k).start()
        return unused

    def end_norm(k, unused):
        recv_norm(k).wait_recv()
        return unused

    def end_send(k, unused):
        send_norm(k).wait_send()
        return unused

    lax.fori_loop(1, PEERS, start_norm, 0)
    lax.fori_loop(1, PEERS, end_norm, 0)
    total = norms[0]
    for k in range(1, PEERS):
        total += norms[k]
    factor = jnp.sqrt(total[0:1, 0:1] / (total[1:2, 0:1] + 1e-06))
    out[0, 0] = (full[...] * factor).astype(jnp.bfloat16)
    out[0, 1] = (last * factor).astype(jnp.bfloat16)

    lax.fori_loop(1, PEERS, end_send, 0)
    for slot in range(2):
        @pl.when(role[slot] != 0)
        def _():
            for index in range(PARTS):
                send_near(slot, 0, index).wait_send()

    @pl.when(is_root)
    def _():
        for index in range(PARTS):
            send_across(index).wait_send()
            for k in range(3):
                send_fresh(lead_slot, 1, k, index).wait_send()

    @pl.when(is_leaf_leader)
    def _():
        for index in range(PARTS):
            send_far(0, index).wait_send()

    @pl.when(leads)
    def _():
        for index in range(PARTS):
            for k in range(3):
                send_fresh(lead_slot, 1, 3 + k, index).wait_send()


def body(grads, order, offset, prev_roots):
    bf16, f32 = jnp.bfloat16, jnp.float32
    dma = pltpu.SemaphoreType.DMA
    return pl.pallas_call(
        kernel,
        out_shape=jax.ShapeDtypeStruct((1, 2, N, N), bf16),
        in_specs=[
            pl.BlockSpec(memory_space=pltpu.SMEM),
            pl.BlockSpec(memory_space=pltpu.SMEM),
            pl.BlockSpec(memory_space=pltpu.VMEM),
            pl.BlockSpec(memory_space=pl.ANY),
        ],
        out_specs=pl.BlockSpec(memory_space=pltpu.VMEM),
        scratch_shapes=[
            pltpu.VMEM((4, N, N), bf16),
            pltpu.VMEM((2, ROWS, T), f32),
            pltpu.VMEM((ROWS, T), bf16),
            pltpu.VMEM((2, ROWS, T), bf16),
            pltpu.VMEM((3, ROWS, T), bf16),
            pltpu.VMEM((3, ROWS, T), bf16),
            pltpu.VMEM((ROWS, T), bf16),
            pltpu.VMEM((2, ROWS, T), bf16),
            pltpu.VMEM((N, N), f32),
            pltpu.VMEM((ROWS, T), f32),
            pltpu.VMEM((2, N, N), bf16),
            pltpu.VMEM((PEERS, 8, T), f32),
            dma,
            dma((2, PARTS)), dma((3, PARTS)),
            dma((PARTS,)), dma((3, PARTS)),
            dma((PARTS,)), dma((PARTS,)),
            dma((6, PARTS)), dma((2, PARTS)),
            dma((PEERS,)), dma((PEERS,)),
        ],
        compiler_params=pltpu.CompilerParams(
            collective_id=0, has_side_effects=True, vmem_limit_bytes=48 * 1024 * 1024),
        cost_estimate=pl.CostEstimate(flops=10 * 2 * N ** 3, bytes_accessed=4 * 1024 * 1024, transcendentals=0),
        name="refresh",
    )(order, offset, grads, prev_roots)


def solution(mesh):
    placed = (P("dp", "mp", None, None), P("mp", None), P("mp"), P("mp", None, None))
    return jax.shard_map(
        body, mesh=mesh, in_specs=placed, out_specs=P("dp", "mp", None, None), check_vma=False
    )
```

time: 620 us -> 85 us (0.14)
  waiting for transfers between devices: 511 us -> 0 us
  Pallas kernels: 0 us -> 79.7 us
  blocking collectives: 54 us -> 0 us
  matrix products: 26.7 us -> 0 us
  between operations: 15.5 us -> 0.67 us
  other arithmetic: 8.49 us -> 0 us
    psum x2 -> x0, waiting for transfers between devices: 511 us -> none  [the longest x1 256 us: from_root(): return lax.psum(block, axis)]
    pallas_call x0 -> x1, Pallas kernels: none -> 79.7 us  [body(): pl.pallas_call(kernel, out_shape=jax.ShapeDtypeStruct((1, 2, N, N), bf16)...]
    psum x1 -> x0, blocking collectives: 54 us -> none  [body(): grad_total, pre_total = lax.psum((grad_sq, pre_sq), 'mp')]
    dot_general x11 -> x0, matrix products: 26.7 us -> none  [the longest x9 20.1 us: product(): return jnp.dot(first, second, precision=lax.Precision.HIGHEST)]
  transfers between devices with their start and end apart: 2 -> 0, of which waited for: 2 -> 0; matrix products, arithmetic and copies ran while one was open for 0% -> 0% of each run, Pallas kernels for 0% -> 0%
where the time goes in v1:
time: 85 us; the launch traced here: 84.8 us
  Pallas kernels  79.7 us (94%)
  local copies, waits for them, and re-layouts  4.44 us (5%)
    pallas_call x1, Pallas kernels, body(): pl.pallas_call(kernel, out_shape=jax.ShapeDtypeStruct((1, 2, N, N), bf16)...  79.7 us
    unnamed x7, local copies, waits for them, and re-layouts  4.44 us

profile of v1, /device:TPU:1, one launch (start us, length us, event | category | flops | bytes accessed | tf_op | source)
XLA Modules:
  0.0 84.8 jit_solution(6356512483586223577)
XLA Ops:
  0.7 0.0 copy-start
  0.7 1.6 %copy-done = bf16[4,512,512]{2,1,0:T(8,128)(2,1)S(1)} copy-done((bf16[4,512,512]{2,1,0:T(8,128)(2,1)S(1)}, bf16[4,512,512]{2,1,0:T(8,128)(2,1)}, u32[]{:S(2)}) %copy-start) | copy-done | bytes 2097176
  2.2 0.0 copy-start.1
  2.2 1.2 %copy-done.1 = bf16[1,2,512,512]{3,2,1,0:T(8,128)(2,1)S(1)} copy-done((bf16[1,2,512,512]{3,2,1,0:T(8,128)(2,1)S(1)}, bf16[1,2,512,512]{3,2,1,0:T(8,128)(2,1)}, u32[]{:S(2)}) %copy-start.1) | copy-done | bytes 1048600
  3.5 0.0 copy-start.2
  3.5 0.7 copy-done.2
  4.1 79.7 %refresh.1 = bf16[1,2,512,512]{3,2,1,0:T(8,128)(2,1)S(1)} custom-call(s32[1,4]{1,0:T(1,128)S(1)} %copy-done.2, s32[1]{0:T(128)S(6)} %copy.6.offset, bf16[1,2,512,512]{3,2,1,0:T(8,128)(2,1)S(1)} %copy-done.1, bf16[4,512,512]{2,1,0:T(8,128)(2,1)S(1)} %copy-done), custom_call_target="tpu_custom_call" | custom-call | flops 2684354560 | bytes 4194304 | tf_op jit(solution)/shard_map/refresh/pallas_call | solution.py:278
  83.9 1.0 %copy.7 = bf16[1,2,512,512]{3,2,1,0:T(8,128)(2,1)} copy(bf16[1,2,512,512]{3,2,1,0:T(8,128)(2,1)S(1)} %refresh.1) | data formatting | bytes 2097152
Async XLA Ops:
  0.7 1.6 %copy-start = (bf16[4,512,512]{2,1,0:T(8,128)(2,1)S(1)}, bf16[4,512,512]{2,1,0:T(8,128)(2,1)}, u32[]{:S(2)}) copy-start(bf16[4,512,512]{2,1,0:T(8,128)(2,1)} %prev.1) | copy-start | bytes 6291460
  2.2 1.2 %copy-start.1 = (bf16[1,2,512,512]{3,2,1,0:T(8,128)(2,1)S(1)}, bf16[1,2,512,512]{3,2,1,0:T(8,128)(2,1)}, u32[]{:S(2)}) copy-start(bf16[1,2,512,512]{3,2,1,0:T(8,128)(2,1)} %grads.1) | copy-start | bytes 3145732
  3.5 0.7 copy-start.2

commit v2 on v1

v2 whole, which is shorter than its diff:
```python
import jax
import jax.numpy as jnp
from jax import lax
from jax.experimental import pallas as pl
from jax.experimental.pallas import tpu as pltpu
from jax.sharding import PartitionSpec as P

MESH = pl.DeviceIdType.MESH
N = 512
T = 128
REPLICAS = 32
RING = 16
PEERS = 16
RIDGE = 0.1
ABOVE = (((0, 1), (0, 2), (0, 3)), ((1, 2), (1, 3), (2, 3)))
HALF = 4 * T + 16
PARTS = ((0, 256), (256, 272))
MEMBERS = (1, 2, -1)
LEADERS = (4, -4, 8)
GREETED = 7 + 5 + PEERS - 1


def part(index):
    return pl.ds(*PARTS[index])


def small(a, b):
    return jnp.dot(a.astype(jnp.bfloat16), b.astype(jnp.bfloat16), preferred_element_type=jnp.float32)


def total_square(value):
    return jnp.sum(jnp.sum(value * value, axis=0, keepdims=True), axis=1, keepdims=True)


def positions(rows, columns):
    shape = (rows, columns)
    return lax.broadcasted_iota(jnp.int32, shape, 0), lax.broadcasted_iota(jnp.int32, shape, 1)


def pack(top, bottom, store):
    row, column = positions(T, T)
    for h in range(2):
        tile = lambda i, j: (top[i * T:(i + 1) * T, j * T:(j + 1) * T] if i < 2 else
                             bottom[(i - 2) * T:(i - 1) * T, (j - 2) * T:(j - 1) * T])
        first, second = tile(2 * h, 2 * h), tile(2 * h + 1, 2 * h + 1)
        store(h, 0, jnp.where(column >= row, first, second))
        for index, (i, j) in enumerate(ABOVE[h]):
            store(h, (index + 1) * T, tile(i, j))
        diagonal = jnp.sum(jnp.where(column == row, second, 0.0), axis=0, keepdims=True)
        store(h, 4 * T, jnp.broadcast_to(diagonal, (16, T)))


def unpack(packed, full):
    row, column = positions(T, T)
    for h in range(2):
        both = packed[h, 0:T, :].astype(jnp.float32)
        mirrored = both.T
        diagonal = packed[h, 4 * T:4 * T + 16, :].astype(jnp.float32)[0:1]
        first = jnp.where(column >= row, both, mirrored)
        second = jnp.where(column < row, both, jnp.where(column == row, diagonal, mirrored))
        for block, i in ((first, 2 * h), (second, 2 * h + 1)):
            full[i * T:(i + 1) * T, i * T:(i + 1) * T] = block.astype(full.dtype)
        for index, (i, j) in enumerate(ABOVE[h]):
            block = packed[h, (index + 1) * T:(index + 2) * T, :]
            full[i * T:(i + 1) * T, j * T:(j + 1) * T] = block
            full[j * T:(j + 1) * T, i * T:(i + 1) * T] = block.T


def next_state(a):
    e2 = (small(a, a) - 10.0 * a) * 0.0625
    e4 = 3.125 * e2 + small(e2, e2)
    return 2.44140625 * a + small(e4, a)


def inverse_root(stat):
    row, column = positions(N, N)
    eye = jnp.where(row == column, 1.0, 0.0)
    ridged = stat * (1.0 / (N * REPLICAS)) + RIDGE * eye
    start = 2.5 / jnp.sqrt(total_square(ridged))
    a = start * ridged
    b = next_state(a)
    c = next_state(b)
    g = small(a, b) * 0.0625 - 0.3125 * (a + b)
    scale = jnp.sqrt(jnp.sqrt(start))
    top, bottom = (
        scale * (1.953125 * eye[rows, columns] + 1.25 * g[rows, columns] - 0.390625 * c[rows, columns]
                 - 0.25 * small(g[rows], c[:, columns]))
        for rows, columns in ((slice(0, 256), slice(0, N)), (slice(256, N), slice(256, N))))
    return top, bottom


def kernel(order, offset, grads, prev, out, order_here, offset_here, own, old, stat, sent, near, mine, far, across, both, fresh,
           full, roots, norms, order_sem, offset_sem, own_sem, old_sem, near_send, near_recv, far_send, far_recv, across_send,
           across_recv, fresh_send, fresh_recv, norm_send, norm_recv):
    dp, mp = lax.axis_index("dp"), lax.axis_index("mp")
    z, line, core = dp // 2, dp % 2, mp % 2
    sign = 1 - 2 * core

    loads = [pltpu.make_async_copy(*refs) for refs in (
        (order, order_here, order_sem), (offset, offset_here, offset_sem), (grads, own, own_sem), (prev, old, old_sem))]
    for load in loads:
        load.start()

    def along(step, flip=False):
        there = lax.rem(dp + 2 * step + 2 * RING, 2 * RING)
        return (there + 1 - 2 * line if flip else there, mp)

    barrier = pltpu.get_barrier_semaphore()
    for step in (1, -1, 2, -2, 4, -4, 8):
        pl.semaphore_signal(barrier, inc=1, device_id=along(step), device_id_type=MESH)
    for step in (0, 1, -1, 2, -2):
        pl.semaphore_signal(barrier, inc=1, device_id=along(step, True), device_id_type=MESH)

    def greet(k, unused):
        pl.semaphore_signal(barrier, inc=1, device_id=(dp, lax.rem(mp + k, PEERS)), device_id_type=MESH)
        return unused

    lax.fori_loop(1, PEERS, greet, 0)

    place = [lax.rem(sign * (z - 5 * (2 * slot + core)) + 8 * RING, RING) for slot in range(2)]
    role = [lax.rem(p, 4) for p in place]
    leads = jnp.logical_or(role[0] == 0, role[1] == 0)
    lead_slot = jnp.where(role[1] == 0, 1, 0)
    lead_place = jnp.where(role[1] == 0, place[1], place[0])
    is_root = jnp.logical_and(leads, lead_place == 0)
    passes_on = jnp.logical_and(leads, lead_place != 0)

    def remote(source, target, send_sem, recv_sem, device):
        return pltpu.make_async_remote_copy(
            src_ref=source, dst_ref=target, send_sem=send_sem, recv_sem=recv_sem, device_id=device, device_id_type=MESH)

    def send_near(slot, k, index):
        half = line if k < 3 else 1 - line
        device = along(0 if k == 6 else -sign * MEMBERS[k % 3], k >= 3)
        return remote(sent.at[slot, half, part(index)], near.at[k, part(index)],
                      near_send.at[slot, 0 if k < 3 else 1, index], near_recv.at[k, index], device)

    def send_far(k, index):
        return remote(mine.at[part(index)], far.at[k, part(index)], far_send.at[index], far_recv.at[k, index],
                      along(-sign * LEADERS[k]))

    def send_across(index):
        return remote(mine.at[part(index)], across.at[part(index)], across_send.at[index], across_recv.at[index],
                      along(0, True))

    def send_fresh(slot, half, k, index):
        step = 0 if k == 9 else sign * (LEADERS + MEMBERS + MEMBERS)[k]
        return remote(fresh.at[slot, half, part(index)], fresh.at[slot, half, part(index)], fresh_send.at[k, index],
                      fresh_recv.at[slot, half, index], along(step, k >= 6))

    loads[0].wait()
    loads[1].wait()
    items = [order_here[0, (offset_here[0] + slot) % 4] for slot in range(2)]
    loads[2].wait()
    for slot in range(2):
        item = items[slot]
        picked = own[0, item // 2]
        turned = jnp.where(item % 2 == 0, picked, picked.T)
        top, bottom = (
            lax.dot_general(a, b, (((1,), (1,)), ((), ())), preferred_element_type=jnp.float32)
            for a, b in ((turned[:256], turned), (turned[256:], turned[256:])))

        def keep(h, first, rows):
            stat[slot, h, first:first + rows.shape[0], :] = rows
            sent[slot, h, first:first + rows.shape[0], :] = rows.astype(jnp.bfloat16)

        pack(top, bottom, keep)
        if slot == 0:
            pl.semaphore_wait(barrier, GREETED)
        for k in range(3):
            @pl.when(role[slot] == k + 1)
            def _():
                for index in range(len(PARTS)):
                    send_near(slot, k, index).start()
                    send_near(slot, k + 3, index).start()

        @pl.when(role[slot] == 0)
        def _():
            for index in range(len(PARTS)):
                send_near(slot, 6, index).start()

    grad_sq = total_square(own[0, 0].astype(jnp.float32)) + total_square(own[0, 1].astype(jnp.float32))

    @pl.when(leads)
    def _():
        for index in range(len(PARTS)):
            for k in range(7):
                send_near(0, k, index).wait_recv()
            total = stat[lead_slot, line, part(index)]
            for k in range(7):
                total += near[k, part(index)].astype(jnp.float32)
            both[line, part(index)] = total
            mine[part(index)] = total.astype(jnp.bfloat16)
            for k in range(3):
                @pl.when(lead_place == LEADERS[k] % RING)
                def _():
                    send_far(k, index).start()

    @pl.when(is_root)
    def _():
        for index in range(len(PARTS)):
            for k in range(3):
                send_far(k, index).wait_recv()
            total = both[line, part(index)]
            for k in range(3):
                total += far[k, part(index)].astype(jnp.float32)
            both[line, part(index)] = total
            mine[part(index)] = total.astype(jnp.bfloat16)
            send_across(index).start()
        for index in range(len(PARTS)):
            send_across(index).wait_recv()
            both[1 - line, part(index)] = across[part(index)].astype(jnp.float32)
        unpack(both, full)
        top, bottom = inverse_root(full[...])

        def keep(h, first, rows):
            fresh[lead_slot, h, first:first + rows.shape[0], :] = rows.astype(jnp.bfloat16)

        pack(top, bottom, keep)
        for index in range(len(PARTS)):
            for k in range(9):
                send_fresh(lead_slot, line, k, index).start()

    @pl.when(passes_on)
    def _():
        for index in range(len(PARTS)):
            send_fresh(lead_slot, line, 0, index).wait_recv()
            for k in range(3, 10):
                send_fresh(lead_slot, line, k, index).start()

    loads[3].wait()
    for slot in range(2):
        for half in range(2):
            @pl.when(jnp.logical_or(role[slot] != 0, jnp.logical_and(place[slot] != 0, line != half)))
            def _():
                for index in range(len(PARTS)):
                    send_fresh(slot, half, 0, index).wait_recv()
        unpack(fresh.at[slot], roots.at[slot])

    pre_sq = jnp.zeros((1, 1), jnp.float32)
    unscaled = []
    for b in range(2):
        left, right = (
            jnp.where(items[0] == k, roots[0], jnp.where(items[1] == k, roots[1], old[k])) for k in (2 * b, 2 * b + 1))
        done = jnp.dot(left, own[0, b], preferred_element_type=jnp.float32).astype(jnp.bfloat16)
        unscaled.append(jnp.dot(done, right, preferred_element_type=jnp.float32))
        pre_sq += total_square(unscaled[b])

    norms[mp] = jnp.where(positions(8, T)[0] == 0, grad_sq, pre_sq)

    def send_norm(k):
        return remote(norms.at[mp], norms.at[mp], norm_send.at[k], norm_recv.at[mp], (dp, lax.rem(mp + k, PEERS)))

    def recv_norm(k):
        source = lax.rem(mp + k, PEERS)
        return remote(norms.at[source], norms.at[source], norm_send.at[k], norm_recv.at[source], (dp, source))

    def start_norm(k, unused):
        send_norm(k).start()
        return unused

    def end_norm(k, unused):
        recv_norm(k).wait_recv()
        return unused

    def end_send(k, unused):
        send_norm(k).wait_send()
        return unused

    lax.fori_loop(1, PEERS, start_norm, 0)
    lax.fori_loop(1, PEERS, end_norm, 0)
    total = norms[0]
    for k in range(1, PEERS):
        total += norms[k]
    factor = jnp.sqrt(total[0:1, 0:1] / (total[1:2, 0:1] + 1e-06))
    for b in range(2):
        out[0, b] = (unscaled[b] * factor).astype(jnp.bfloat16)

    lax.fori_loop(1, PEERS, end_send, 0)
    for index in range(len(PARTS)):
        for slot in range(2):
            @pl.when(role[slot] != 0)
            def _():
                send_near(slot, 0, index).wait_send()
            send_near(slot, 3, index).wait_send()

        @pl.when(is_root)
        def _():
            send_across(index).wait_send()
            for k in range(9):
                send_fresh(lead_slot, line, k, index).wait_send()

        @pl.when(passes_on)
        def _():
            send_far(0, index).wait_send()
            for k in range(3, 10):
                send_fresh(lead_slot, line, k, index).wait_send()


def body(grads, order, offset, prev_roots):
    bf16, f32 = jnp.bfloat16, jnp.float32
    dma, parts = pltpu.SemaphoreType.DMA, len(PARTS)
    return pl.pallas_call(
        kernel,
        out_shape=jax.ShapeDtypeStruct((1, 2, N, N), bf16),
        in_specs=[pl.BlockSpec(memory_space=pl.ANY)] * 4,
        out_specs=pl.BlockSpec(memory_space=pltpu.VMEM),
        scratch_shapes=[
            pltpu.SMEM((1, 4), jnp.int32),
            pltpu.SMEM((1,), jnp.int32),
            pltpu.VMEM((1, 2, N, N), bf16),
            pltpu.VMEM((4, N, N), bf16),
            pltpu.VMEM((2, 2, HALF, T), f32),
            pltpu.VMEM((2, 2, HALF, T), bf16),
            pltpu.VMEM((7, HALF, T), bf16),
            pltpu.VMEM((HALF, T), bf16),
            pltpu.VMEM((3, HALF, T), bf16),
            pltpu.VMEM((HALF, T), bf16),
            pltpu.VMEM((2, HALF, T), f32),
            pltpu.VMEM((2, 2, HALF, T), bf16),
            pltpu.VMEM((N, N), f32),
            pltpu.VMEM((2, N, N), bf16),
            pltpu.VMEM((PEERS, 8, T), f32),
            dma, dma, dma, dma,
            dma((2, 2, parts)), dma((7, parts)),
            dma((parts,)), dma((3, parts)),
            dma((parts,)), dma((parts,)),
            dma((10, parts)), dma((2, 2, parts)),
            dma((PEERS,)), dma((PEERS,)),
        ],
        compiler_params=pltpu.CompilerParams(
            collective_id=0, has_side_effects=True, vmem_limit_bytes=60 * 1024 * 1024),
        cost_estimate=pl.CostEstimate(flops=10 * 2 * N ** 3, bytes_accessed=4 * 1024 * 1024, transcendentals=0),
        name="refresh",
    )(order, offset, grads, prev_roots)


def solution(mesh):
    placed = (P("dp", "mp", None, None), P("mp", None), P("mp"), P("mp", None, None))
    return jax.shard_map(
        body, mesh=mesh, in_specs=placed, out_specs=P("dp", "mp", None, None), check_vma=False
    )
```

time: 85 us -> 70.6 us (0.83)
  Pallas kernels: 79.7 us -> 67.5 us
  local copies, waits for them, and re-layouts: 4.44 us -> 2.26 us
    pallas_call x1, Pallas kernels: 79.7 us -> 67.5 us  [body(): pl.pallas_call(kernel, out_shape=jax.ShapeDtypeStruct((1, 2, N, N), bf16)...]
    unnamed x7 -> x1, local copies, waits for them, and re-layouts: 4.44 us -> 2.26 us
where the time goes in v2:
time: 70.6 us; the launch traced here: 70.4 us
  Pallas kernels  67.5 us (96%)
  local copies, waits for them, and re-layouts  2.26 us (3%)
    pallas_call x1, Pallas kernels, body(): pl.pallas_call(kernel, out_shape=jax.ShapeDtypeStruct((1, 2, N, N), bf16)...  67.5 us
    unnamed x1, local copies, waits for them, and re-layouts  2.26 us

profile of v2, /device:TPU:1, one launch (start us, length us, event | category | flops | bytes accessed | tf_op | source)
XLA Modules:
  0.0 70.4 jit_solution(15447542528538178950)
XLA Ops:
  0.7 67.5 %refresh.1 = bf16[1,2,512,512]{3,2,1,0:T(8,128)(2,1)} custom-call(s32[1,4]{1,0:T(1,128)} %order.1, s32[1]{0:T(128)S(6)} %copy.6.offset, bf16[1,2,512,512]{3,2,1,0:T(8,128)(2,1)} %grads.1, bf16[4,512,512]{2,1,0:T(8,128)(2,1)} %prev.1), custom_call_target="tpu_custom_call" | custom-call | flops 2684354560 | bytes 4194304 | tf_op jit(solution)/shard_map/refresh/pallas_call | solution.py:303
  68.2 2.3 %copy.7 = bf16[1,2,512,512]{3,2,1,0:T(8,128)(2,1)} copy(bf16[1,2,512,512]{3,2,1,0:T(8,128)(2,1)} %refresh.1) | data formatting | bytes 2097152

commit v3 on v2

--- a/solution.py
+++ b/solution.py
@@ -17,7 +17,8 @@
 PARTS = ((0, 256), (256, 272))
 MEMBERS = (1, 2, -1)
 LEADERS = (4, -4, 8)
-GREETED = 7 + 5 + PEERS - 1
+NORM_PEERS = [(1, 2, 1), (1, 2, 0), (1, 1, 1), (1, 3, 1), (1, 1, 0), (1, 3, 0), (1, 0, 1), (1, 0, 0),
+              (0, 2, 1), (0, 2, 0), (0, 1, 1), (0, 3, 1), (0, 1, 0), (0, 3, 0), (0, 0, 1)]
 
 
 def part(index):
@@ -89,9 +90,9 @@
     return top, bottom
 
 
-def kernel(order, offset, grads, prev, out, order_here, offset_here, own, old, stat, sent, near, mine, far, across, both, fresh,
+def kernel(order, offset, grads, prev, out, order_here, offset_here, own, old, stat, sent, near, mine, mine_all, far, across, both, fresh,
            full, roots, norms, order_sem, offset_sem, own_sem, old_sem, near_send, near_recv, far_send, far_recv, across_send,
-           across_recv, fresh_send, fresh_recv, norm_send, norm_recv):
+           across_recv, fresh_send, fresh_recv, norm_send, norm_recv, four_ready, eight_ready, peers_ready):
     dp, mp = lax.axis_index("dp"), lax.axis_index("mp")
     z, line, core = dp // 2, dp % 2, mp % 2
     sign = 1 - 2 * core
@@ -105,25 +106,21 @@
         there = lax.rem(dp + 2 * step + 2 * RING, 2 * RING)
         return (there + 1 - 2 * line if flip else there, mp)
 
+    def peer(y_step, x_step, core_step):
+        return (dp, (1 - mp // 8 if y_step else mp // 8) * 8 + (mp // 2 + x_step) % 4 * 2 + (1 - core if core_step else core))
+
+    def signal(semaphore, device):
+        pl.semaphore_signal(semaphore, inc=1, device_id=device, device_id_type=MESH)
+
     barrier = pltpu.get_barrier_semaphore()
-    for step in (1, -1, 2, -2, 4, -4, 8):
-        pl.semaphore_signal(barrier, inc=1, device_id=along(step), device_id_type=MESH)
-    for step in (0, 1, -1, 2, -2):
-        pl.semaphore_signal(barrier, inc=1, device_id=along(step, True), device_id_type=MESH)
-
-    def greet(k, unused):
-        pl.semaphore_signal(barrier, inc=1, device_id=(dp, lax.rem(mp + k, PEERS)), device_id_type=MESH)
-        return unused
-
-    lax.fori_loop(1, PEERS, greet, 0)
-
-    place = [lax.rem(sign * (z - 5 * (2 * slot + core)) + 8 * RING, RING) for slot in range(2)]
-    role = [lax.rem(p, 4) for p in place]
+    greeted = [along(step) for step in (2, -2, 1, -1)] + [along(step, True) for step in (2, -2, 1, -1, 0)]
+    greeted += [peer(1, 0, 0)] + [peer(*steps) for steps in NORM_PEERS if not steps[0]]
+    for device in greeted:
+        signal(barrier, device)
+
+    role = [(sign * (z - 2 * slot - core) + 2 * RING) % 4 for slot in range(2)]
     leads = jnp.logical_or(role[0] == 0, role[1] == 0)
     lead_slot = jnp.where(role[1] == 0, 1, 0)
-    lead_place = jnp.where(role[1] == 0, place[1], place[0])
-    is_root = jnp.logical_and(leads, lead_place == 0)
-    passes_on = jnp.logical_and(leads, lead_place != 0)
 
     def remote(source, target, send_sem, recv_sem, device):
         return pltpu.make_async_remote_copy(
@@ -136,17 +133,16 @@
                       near_send.at[slot, 0 if k < 3 else 1, index], near_recv.at[k, index], device)
 
     def send_far(k, index):
-        return remote(mine.at[part(index)], far.at[k, part(index)], far_send.at[index], far_recv.at[k, index],
-                      along(-sign * LEADERS[k]))
+        return remote(mine.at[part(index)], far.at[k, part(index)], far_send.at[k, index], far_recv.at[k, index],
+                      along(LEADERS[k]))
 
     def send_across(index):
-        return remote(mine.at[part(index)], across.at[part(index)], across_send.at[index], across_recv.at[index],
+        return remote(mine_all.at[part(index)], across.at[part(index)], across_send.at[index], across_recv.at[index],
                       along(0, True))
 
     def send_fresh(slot, half, k, index):
-        step = 0 if k == 9 else sign * (LEADERS + MEMBERS + MEMBERS)[k]
         return remote(fresh.at[slot, half, part(index)], fresh.at[slot, half, part(index)], fresh_send.at[k, index],
-                      fresh_recv.at[slot, half, index], along(step, k >= 6))
+                      fresh_recv.at[slot, half, index], along(sign * MEMBERS[k % 3], k >= 3))
 
     loads[0].wait()
     loads[1].wait()
@@ -166,7 +162,7 @@
 
         pack(top, bottom, keep)
         if slot == 0:
-            pl.semaphore_wait(barrier, GREETED)
+            pl.semaphore_wait(barrier, len(greeted))
         for k in range(3):
             @pl.when(role[slot] == k + 1)
             def _():
@@ -179,7 +175,14 @@
             for index in range(len(PARTS)):
                 send_near(slot, 6, index).start()
 
+    for step in (2, -2):
+        signal(four_ready, along(step))
+    signal(peers_ready, peer(1, 0, 0))
     grad_sq = total_square(own[0, 0].astype(jnp.float32)) + total_square(own[0, 1].astype(jnp.float32))
+    pl.semaphore_wait(four_ready, 2)
+    for step in (4, -4):
+        signal(eight_ready, along(step))
+    pl.semaphore_wait(eight_ready, 2)
 
     @pl.when(leads)
     def _():
@@ -191,13 +194,8 @@
                 total += near[k, part(index)].astype(jnp.float32)
             both[line, part(index)] = total
             mine[part(index)] = total.astype(jnp.bfloat16)
-            for k in range(3):
-                @pl.when(lead_place == LEADERS[k] % RING)
-                def _():
-                    send_far(k, index).start()
-
-    @pl.when(is_root)
-    def _():
+            for k in (2, 0, 1):
+                send_far(k, index).start()
         for index in range(len(PARTS)):
             for k in range(3):
                 send_far(k, index).wait_recv()
@@ -205,7 +203,7 @@
             for k in range(3):
                 total += far[k, part(index)].astype(jnp.float32)
             both[line, part(index)] = total
-            mine[part(index)] = total.astype(jnp.bfloat16)
+            mine_all[part(index)] = total.astype(jnp.bfloat16)
             send_across(index).start()
         for index in range(len(PARTS)):
             send_across(index).wait_recv()
@@ -218,22 +216,15 @@
 
         pack(top, bottom, keep)
         for index in range(len(PARTS)):
-            for k in range(9):
-                send_fresh(lead_slot, line, k, index).start()
-
-    @pl.when(passes_on)
-    def _():
-        for index in range(len(PARTS)):
-            send_fresh(lead_slot, line, 0, index).wait_recv()
-            for k in range(3, 10):
+            for k in range(6):
                 send_fresh(lead_slot, line, k, index).start()
 
     loads[3].wait()
     for slot in range(2):
-        for half in range(2):
-            @pl.when(jnp.logical_or(role[slot] != 0, jnp.logical_and(place[slot] != 0, line != half)))
-            def _():
-                for index in range(len(PARTS)):
+        @pl.when(role[slot] != 0)
+        def _():
+            for index in range(len(PARTS)):
+                for half in range(2):
                     send_fresh(slot, half, 0, index).wait_recv()
         unpack(fresh.at[slot], roots.at[slot])
 
@@ -249,26 +240,17 @@
     norms[mp] = jnp.where(positions(8, T)[0] == 0, grad_sq, pre_sq)
 
     def send_norm(k):
-        return remote(norms.at[mp], norms.at[mp], norm_send.at[k], norm_recv.at[mp], (dp, lax.rem(mp + k, PEERS)))
+        return remote(norms.at[mp], norms.at[mp], norm_send.at[k], norm_recv.at[mp], peer(*NORM_PEERS[k]))
 
     def recv_norm(k):
-        source = lax.rem(mp + k, PEERS)
-        return remote(norms.at[source], norms.at[source], norm_send.at[k], norm_recv.at[source], (dp, source))
-
-    def start_norm(k, unused):
+        device = peer(*NORM_PEERS[k])
+        return remote(norms.at[device[1]], norms.at[device[1]], norm_send.at[k], norm_recv.at[device[1]], device)
+
+    pl.semaphore_wait(peers_ready, 1)
+    for k in range(PEERS - 1):
         send_norm(k).start()
-        return unused
-
-    def end_norm(k, unused):
+    for k in range(PEERS - 1):
         recv_norm(k).wait_recv()
-        return unused
-
-    def end_send(k, unused):
-        send_norm(k).wait_send()
-        return unused
-
-    lax.fori_loop(1, PEERS, start_norm, 0)
-    lax.fori_loop(1, PEERS, end_norm, 0)
     total = norms[0]
     for k in range(1, PEERS):
         total += norms[k]
@@ -276,7 +258,8 @@
     for b in range(2):
         out[0, b] = (unscaled[b] * factor).astype(jnp.bfloat16)
 
-    lax.fori_loop(1, PEERS, end_send, 0)
+    for k in range(PEERS - 1):
+        send_norm(k).wait_send()
     for index in range(len(PARTS)):
         for slot in range(2):
             @pl.when(role[slot] != 0)
@@ -284,16 +267,12 @@
                 send_near(slot, 0, index).wait_send()
             send_near(slot, 3, index).wait_send()
 
-        @pl.when(is_root)
+        @pl.when(leads)
         def _():
             send_across(index).wait_send()
-            for k in range(9):
-                send_fresh(lead_slot, line, k, index).wait_send()
-
-        @pl.when(passes_on)
-        def _():
-            send_far(0, index).wait_send()
-            for k in range(3, 10):
+            for k in range(3):
+                send_far(k, index).wait_send()
+            for k in range(6):
                 send_fresh(lead_slot, line, k, index).wait_send()
 
 
@@ -314,6 +293,7 @@
             pltpu.VMEM((2, 2, HALF, T), bf16),
             pltpu.VMEM((7, HALF, T), bf16),
             pltpu.VMEM((HALF, T), bf16),
+            pltpu.VMEM((HALF, T), bf16),
             pltpu.VMEM((3, HALF, T), bf16),
             pltpu.VMEM((HALF, T), bf16),
             pltpu.VMEM((2, HALF, T), f32),
@@ -323,10 +303,11 @@
             pltpu.VMEM((PEERS, 8, T), f32),
             dma, dma, dma, dma,
             dma((2, 2, parts)), dma((7, parts)),
-            dma((parts,)), dma((3, parts)),
+            dma((3, parts)), dma((3, parts)),
             dma((parts,)), dma((parts,)),
-            dma((10, parts)), dma((2, 2, parts)),
+            dma((6, parts)), dma((2, 2, parts)),
             dma((PEERS,)), dma((PEERS,)),
+            pltpu.SemaphoreType.REGULAR, pltpu.SemaphoreType.REGULAR, pltpu.SemaphoreType.REGULAR,
         ],
         compiler_params=pltpu.CompilerParams(
             collective_id=0, has_side_effects=True, vmem_limit_bytes=60 * 1024 * 1024),

time: 70.6 us -> 65.4 us (0.926)
  Pallas kernels: 67.5 us -> 62.3 us
    pallas_call x1, Pallas kernels: 67.5 us -> 62.3 us  [body(): pl.pallas_call(kernel, out_shape=jax.ShapeDtypeStruct((1, 2, N, N), bf16)...]
where the time goes in v3:
time: 65.4 us; the launch traced here: 65.2 us
  Pallas kernels  62.3 us (95%)
  local copies, waits for them, and re-layouts  2.26 us (3%)
  between operations  0.66 us (1%)
    pallas_call x1, Pallas kernels, body(): pl.pallas_call(kernel, out_shape=jax.ShapeDtypeStruct((1, 2, N, N), bf16)...  62.3 us
    unnamed x1, local copies, waits for them, and re-layouts  2.26 us

profile of v3, /device:TPU:1, one launch (start us, length us, event | category | flops | bytes accessed | tf_op | source)
XLA Modules:
  0.0 65.2 jit_solution(10187505586904280716)
XLA Ops:
  0.7 62.3 %refresh.1 = bf16[1,2,512,512]{3,2,1,0:T(8,128)(2,1)} custom-call(s32[1,4]{1,0:T(1,128)} %order.1, s32[1]{0:T(128)S(6)} %copy.6.offset, bf16[1,2,512,512]{3,2,1,0:T(8,128)(2,1)} %grads.1, bf16[4,512,512]{2,1,0:T(8,128)(2,1)} %prev.1), custom_call_target="tpu_custom_call" | custom-call | flops 2684354560 | bytes 4194304 | tf_op jit(solution)/shard_map/refresh/pallas_call | solution.py:282
  63.0 2.3 %copy.7 = bf16[1,2,512,512]{3,2,1,0:T(8,128)(2,1)} copy(bf16[1,2,512,512]{3,2,1,0:T(8,128)(2,1)} %refresh.1) | data formatting | bytes 2097152

commit v4 on v3

--- a/solution.py
+++ b/solution.py
@@ -14,7 +14,7 @@
 RIDGE = 0.1
 ABOVE = (((0, 1), (0, 2), (0, 3)), ((1, 2), (1, 3), (2, 3)))
 HALF = 4 * T + 16
-PARTS = ((0, 256), (256, 272))
+PARTS = ((0, 208), (208, 176), (384, 144))
 MEMBERS = (1, 2, -1)
 LEADERS = (4, -4, 8)
 NORM_PEERS = [(1, 2, 1), (1, 2, 0), (1, 1, 1), (1, 3, 1), (1, 1, 0), (1, 3, 0), (1, 0, 1), (1, 0, 0),
@@ -141,8 +141,8 @@
                       along(0, True))
 
     def send_fresh(slot, half, k, index):
-        return remote(fresh.at[slot, half, part(index)], fresh.at[slot, half, part(index)], fresh_send.at[k, index],
-                      fresh_recv.at[slot, half, index], along(sign * MEMBERS[k % 3], k >= 3))
+        return remote(fresh.at[slot, half, part(index)], fresh.at[slot, half, part(index)], fresh_send.at[half, k, index],
+                      fresh_recv.at[slot, half, index], along(sign * MEMBERS[k]))
 
     loads[0].wait()
     loads[1].wait()
@@ -215,9 +215,10 @@
             fresh[lead_slot, h, first:first + rows.shape[0], :] = rows.astype(jnp.bfloat16)
 
         pack(top, bottom, keep)
-        for index in range(len(PARTS)):
-            for k in range(6):
-                send_fresh(lead_slot, line, k, index).start()
+        for half in range(2):
+            for index in range(len(PARTS)):
+                for k in range(3):
+                    send_fresh(lead_slot, half, k, index).start()
 
     loads[3].wait()
     for slot in range(2):
@@ -272,8 +273,13 @@
             send_across(index).wait_send()
             for k in range(3):
                 send_far(k, index).wait_send()
-            for k in range(6):
-                send_fresh(lead_slot, line, k, index).wait_send()
+            for half in range(2):
+                for k in range(3):
+                    send_fresh(lead_slot, half, k, index).wait_send()
+
+
+def pinned(array):
+    return pltpu.with_memory_space_constraint(array, pltpu.HBM)
 
 
 def body(grads, order, offset, prev_roots):
@@ -305,15 +311,15 @@
             dma((2, 2, parts)), dma((7, parts)),
             dma((3, parts)), dma((3, parts)),
             dma((parts,)), dma((parts,)),
-            dma((6, parts)), dma((2, 2, parts)),
+            dma((2, 3, parts)), dma((2, 2, parts)),
             dma((PEERS,)), dma((PEERS,)),
             pltpu.SemaphoreType.REGULAR, pltpu.SemaphoreType.REGULAR, pltpu.SemaphoreType.REGULAR,
         ],
         compiler_params=pltpu.CompilerParams(
-            collective_id=0, has_side_effects=True, vmem_limit_bytes=60 * 1024 * 1024),
+            collective_id=0, has_side_effects=True, vmem_limit_bytes=40 * 1024 * 1024),
         cost_estimate=pl.CostEstimate(flops=10 * 2 * N ** 3, bytes_accessed=4 * 1024 * 1024, transcendentals=0),
         name="refresh",
-    )(order, offset, grads, prev_roots)
+    )(pinned(order), offset, pinned(grads), pinned(prev_roots))
 
 
 def solution(mesh):

time: 65.4 us -> 61.9 us (0.946)
  Pallas kernels: 62.3 us -> 60.1 us
  local copies, waits for them, and re-layouts: 2.26 us -> 0.97 us
    pallas_call x1, Pallas kernels: 62.3 us -> 60.1 us  [body(): pl.pallas_call(kernel, out_shape=jax.ShapeDtypeStruct((1, 2, N, N), bf16)...]
    unnamed x1, local copies, waits for them, and re-layouts: 2.26 us -> 0.97 us
where the time goes in v4:
time: 61.9 us; the launch traced here: 61.7 us
  Pallas kernels  60.1 us (97%)
  local copies, waits for them, and re-layouts  0.97 us (2%)
  between operations  0.66 us (1%)
    pallas_call x1, Pallas kernels, body(): pl.pallas_call(kernel, out_shape=jax.ShapeDtypeStruct((1, 2, N, N), bf16)...  60.1 us

profile of v4, /device:TPU:1, one launch (start us, length us, event | category | flops | bytes accessed | tf_op | source)
XLA Modules:
  0.0 61.7 jit_solution(10326632107421494603)
XLA Ops:
  0.7 60.1 %refresh.1 = bf16[1,2,512,512]{3,2,1,0:T(8,128)(2,1)S(1)} custom-call(s32[1,4]{1,0:T(1,128)} %order.1, s32[1]{0:T(128)S(6)} %copy.6.offset, bf16[1,2,512,512]{3,2,1,0:T(8,128)(2,1)} %grads.1, bf16[4,512,512]{2,1,0:T(8,128)(2,1)} %prev.1), custom_call_target="tpu_custom_call" | custom-call | flops 2684354560 | bytes 4194304 | tf_op jit(solution)/shard_map/refresh/pallas_call | solution.py:288
  60.8 1.0 %copy.7 = bf16[1,2,512,512]{3,2,1,0:T(8,128)(2,1)} copy(bf16[1,2,512,512]{3,2,1,0:T(8,128)(2,1)S(1)} %refresh.1) | data formatting | bytes 2097152

commit v5 on v4

--- a/solution.py
+++ b/solution.py
@@ -16,7 +16,6 @@
 HALF = 4 * T + 16
 PARTS = ((0, 208), (208, 176), (384, 144))
 MEMBERS = (1, 2, -1)
-LEADERS = (4, -4, 8)
 NORM_PEERS = [(1, 2, 1), (1, 2, 0), (1, 1, 1), (1, 3, 1), (1, 1, 0), (1, 3, 0), (1, 0, 1), (1, 0, 0),
               (0, 2, 1), (0, 2, 0), (0, 1, 1), (0, 3, 1), (0, 1, 0), (0, 3, 0), (0, 0, 1)]
 
@@ -90,9 +89,9 @@
     return top, bottom
 
 
-def kernel(order, offset, grads, prev, out, order_here, offset_here, own, old, stat, sent, near, mine, mine_all, far, across, both, fresh,
+def kernel(order, offset, grads, prev, out, order_here, offset_here, own, old, stat, sent, near, mine, far, across, both, fresh,
            full, roots, norms, order_sem, offset_sem, own_sem, old_sem, near_send, near_recv, far_send, far_recv, across_send,
-           across_recv, fresh_send, fresh_recv, norm_send, norm_recv, four_ready, eight_ready, peers_ready):
+           across_recv, fresh_send, fresh_recv, norm_send, norm_recv, four_ready, peers_ready):
     dp, mp = lax.axis_index("dp"), lax.axis_index("mp")
     z, line, core = dp // 2, dp % 2, mp % 2
     sign = 1 - 2 * core
@@ -132,12 +131,14 @@
         return remote(sent.at[slot, half, part(index)], near.at[k, part(index)],
                       near_send.at[slot, 0 if k < 3 else 1, index], near_recv.at[k, index], device)
 
+    first_side = 4 - 8 * ((z // 4 + core) % 2)
+
     def send_far(k, index):
-        return remote(mine.at[part(index)], far.at[k, part(index)], far_send.at[k, index], far_recv.at[k, index],
-                      along(LEADERS[k]))
+        return remote(mine.at[k, part(index)], far.at[k, part(index)], far_send.at[k, index], far_recv.at[k, index],
+                      along(first_side if k == 0 else -first_side))
 
     def send_across(index):
-        return remote(mine_all.at[part(index)], across.at[part(index)], across_send.at[index], across_recv.at[index],
+        return remote(mine.at[2, part(index)], across.at[part(index)], across_send.at[index], across_recv.at[index],
                       along(0, True))
 
     def send_fresh(slot, half, k, index):
@@ -180,9 +181,6 @@
     signal(peers_ready, peer(1, 0, 0))
     grad_sq = total_square(own[0, 0].astype(jnp.float32)) + total_square(own[0, 1].astype(jnp.float32))
     pl.semaphore_wait(four_ready, 2)
-    for step in (4, -4):
-        signal(eight_ready, along(step))
-    pl.semaphore_wait(eight_ready, 2)
 
     @pl.when(leads)
     def _():
@@ -193,18 +191,15 @@
             for k in range(7):
                 total += near[k, part(index)].astype(jnp.float32)
             both[line, part(index)] = total
-            mine[part(index)] = total.astype(jnp.bfloat16)
-            for k in (2, 0, 1):
-                send_far(k, index).start()
-        for index in range(len(PARTS)):
-            for k in range(3):
+            mine[0, part(index)] = total.astype(jnp.bfloat16)
+            send_far(0, index).start()
+        for k in range(2):
+            for index in range(len(PARTS)):
                 send_far(k, index).wait_recv()
-            total = both[line, part(index)]
-            for k in range(3):
-                total += far[k, part(index)].astype(jnp.float32)
-            both[line, part(index)] = total
-            mine_all[part(index)] = total.astype(jnp.bfloat16)
-            send_across(index).start()
+                total = both[line, part(index)] + far[k, part(index)].astype(jnp.float32)
+                both[line, part(index)] = total
+                mine[k + 1, part(index)] = total.astype(jnp.bfloat16)
+                (send_far(1, index) if k == 0 else send_across(index)).start()
         for index in range(len(PARTS)):
             send_across(index).wait_recv()
             both[1 - line, part(index)] = across[part(index)].astype(jnp.float32)
@@ -271,7 +266,7 @@
         @pl.when(leads)
         def _():
             send_across(index).wait_send()
-            for k in range(3):
+            for k in range(2):
                 send_far(k, index).wait_send()
             for half in range(2):
                 for k in range(3):
@@ -298,9 +293,8 @@
             pltpu.VMEM((2, 2, HALF, T), f32),
             pltpu.VMEM((2, 2, HALF, T), bf16),
             pltpu.VMEM((7, HALF, T), bf16),
-            pltpu.VMEM((HALF, T), bf16),
-            pltpu.VMEM((HALF, T), bf16),
             pltpu.VMEM((3, HALF, T), bf16),
+            pltpu.VMEM((2, HALF, T), bf16),
             pltpu.VMEM((HALF, T), bf16),
             pltpu.VMEM((2, HALF, T), f32),
             pltpu.VMEM((2, 2, HALF, T), bf16),
@@ -309,11 +303,11 @@
             pltpu.VMEM((PEERS, 8, T), f32),
             dma, dma, dma, dma,
             dma((2, 2, parts)), dma((7, parts)),
-            dma((3, parts)), dma((3, parts)),
+            dma((2, parts)), dma((2, parts)),
             dma((parts,)), dma((parts,)),
             dma((2, 3, parts)), dma((2, 2, parts)),
             dma((PEERS,)), dma((PEERS,)),
-            pltpu.SemaphoreType.REGULAR, pltpu.SemaphoreType.REGULAR, pltpu.SemaphoreType.REGULAR,
+            pltpu.SemaphoreType.REGULAR, pltpu.SemaphoreType.REGULAR,
         ],
         compiler_params=pltpu.CompilerParams(
             collective_id=0, has_side_effects=True, vmem_limit_bytes=40 * 1024 * 1024),

time: 61.9 us -> 59.6 us (0.963)
  Pallas kernels: 60.1 us -> 57.8 us
    pallas_call x1, Pallas kernels: 60.1 us -> 57.8 us  [body(): pl.pallas_call(kernel, out_shape=jax.ShapeDtypeStruct((1, 2, N, N), bf16)...]
where the time goes in v5:
time: 59.6 us; the launch traced here: 59.5 us
  Pallas kernels  57.8 us (97%)
  local copies, waits for them, and re-layouts  0.97 us (2%)
  between operations  0.66 us (1%)
    pallas_call x1, Pallas kernels, body(): pl.pallas_call(kernel, out_shape=jax.ShapeDtypeStruct((1, 2, N, N), bf16)...  57.8 us

profile of v5, /device:TPU:1, one launch (start us, length us, event | category | flops | bytes accessed | tf_op | source)
XLA Modules:
  0.0 59.5 jit_solution(3279760014010141201)
XLA Ops:
  0.7 57.8 %refresh.1 = bf16[1,2,512,512]{3,2,1,0:T(8,128)(2,1)S(1)} custom-call(s32[1,4]{1,0:T(1,128)} %order.1, s32[1]{0:T(128)S(6)} %copy.6.offset, bf16[1,2,512,512]{3,2,1,0:T(8,128)(2,1)} %grads.1, bf16[4,512,512]{2,1,0:T(8,128)(2,1)} %prev.1), custom_call_target="tpu_custom_call" | custom-call | flops 2684354560 | bytes 4194304 | tf_op jit(solution)/shard_map/refresh/pallas_call | solution.py:283
  58.5 1.0 %copy.7 = bf16[1,2,512,512]{3,2,1,0:T(8,128)(2,1)} copy(bf16[1,2,512,512]{3,2,1,0:T(8,128)(2,1)S(1)} %refresh.1) | data formatting | bytes 2097152

commit v6 on v5

--- a/solution.py
+++ b/solution.py
@@ -37,9 +37,9 @@
     return lax.broadcasted_iota(jnp.int32, shape, 0), lax.broadcasted_iota(jnp.int32, shape, 1)
 
 
-def pack(top, bottom, store):
+def pack(top, bottom, store, halves=(0, 1)):
     row, column = positions(T, T)
-    for h in range(2):
+    for h in halves:
         tile = lambda i, j: (top[i * T:(i + 1) * T, j * T:(j + 1) * T] if i < 2 else
                              bottom[(i - 2) * T:(i - 1) * T, (j - 2) * T:(j - 1) * T])
         first, second = tile(2 * h, 2 * h), tile(2 * h + 1, 2 * h + 1)
@@ -66,8 +66,8 @@
             full[j * T:(j + 1) * T, i * T:(i + 1) * T] = block.T
 
 
-def next_state(a):
-    e2 = (small(a, a) - 10.0 * a) * 0.0625
+def next_state(a, square=None):
+    e2 = ((small(a, a) if square is None else square) - 10.0 * a) * 0.0625
     e4 = 3.125 * e2 + small(e2, e2)
     return 2.44140625 * a + small(e4, a)
 
@@ -76,20 +76,19 @@
     row, column = positions(N, N)
     eye = jnp.where(row == column, 1.0, 0.0)
     ridged = stat * (1.0 / (N * REPLICAS)) + RIDGE * eye
+    square = small(ridged, ridged)
     start = 2.5 / jnp.sqrt(total_square(ridged))
     a = start * ridged
-    b = next_state(a)
+    b = next_state(a, (start * start) * square)
     c = next_state(b)
     g = small(a, b) * 0.0625 - 0.3125 * (a + b)
     scale = jnp.sqrt(jnp.sqrt(start))
-    top, bottom = (
-        scale * (1.953125 * eye[rows, columns] + 1.25 * g[rows, columns] - 0.390625 * c[rows, columns]
-                 - 0.25 * small(g[rows], c[:, columns]))
-        for rows, columns in ((slice(0, 256), slice(0, N)), (slice(256, N), slice(256, N))))
-    return top, bottom
-
-
-def kernel(order, offset, grads, prev, out, order_here, offset_here, own, old, stat, sent, near, mine, far, across, both, fresh,
+    for rows, columns in ((slice(0, 256), slice(0, N)), (slice(256, N), slice(256, N))):
+        yield scale * (1.953125 * eye[rows, columns] + 1.25 * g[rows, columns] - 0.390625 * c[rows, columns]
+                       - 0.25 * small(g[rows], c[:, columns]))
+
+
+def kernel(order, offset, grads, prev, out, order_here, offset_here, own, stat, sent, near, mine, far, across, both, fresh,
            full, roots, norms, order_sem, offset_sem, own_sem, old_sem, near_send, near_recv, far_send, far_recv, across_send,
            across_recv, fresh_send, fresh_recv, norm_send, norm_recv, four_ready, peers_ready):
     dp, mp = lax.axis_index("dp"), lax.axis_index("mp")
@@ -97,7 +96,7 @@
     sign = 1 - 2 * core
 
     loads = [pltpu.make_async_copy(*refs) for refs in (
-        (order, order_here, order_sem), (offset, offset_here, offset_sem), (grads, own, own_sem), (prev, old, old_sem))]
+        (order, order_here, order_sem), (offset, offset_here, offset_sem), (grads, own, own_sem), (prev, roots.at[pl.ds(0, 4)], old_sem))]
     for load in loads:
         load.start()
 
@@ -131,7 +130,7 @@
         return remote(sent.at[slot, half, part(index)], near.at[k, part(index)],
                       near_send.at[slot, 0 if k < 3 else 1, index], near_recv.at[k, index], device)
 
-    first_side = 4 - 8 * ((z // 4 + core) % 2)
+    first_side = 4 - 8 * ((z // 4 + lead_slot) % 2)
 
     def send_far(k, index):
         return remote(mine.at[k, part(index)], far.at[k, part(index)], far_send.at[k, index], far_recv.at[k, index],
@@ -141,9 +140,9 @@
         return remote(mine.at[2, part(index)], across.at[part(index)], across_send.at[index], across_recv.at[index],
                       along(0, True))
 
-    def send_fresh(slot, half, k, index):
-        return remote(fresh.at[slot, half, part(index)], fresh.at[slot, half, part(index)], fresh_send.at[half, k, index],
-                      fresh_recv.at[slot, half, index], along(sign * MEMBERS[k]))
+    def send_fresh(slot, half, k):
+        return remote(fresh.at[slot, half], fresh.at[slot, half], fresh_send.at[half, k], fresh_recv.at[slot, half],
+                      along(sign * MEMBERS[k]))
 
     loads[0].wait()
     loads[1].wait()
@@ -204,31 +203,31 @@
             send_across(index).wait_recv()
             both[1 - line, part(index)] = across[part(index)].astype(jnp.float32)
         unpack(both, full)
-        top, bottom = inverse_root(full[...])
+        panels = inverse_root(full[...])
+        top, bottom = next(panels), None
 
         def keep(h, first, rows):
             fresh[lead_slot, h, first:first + rows.shape[0], :] = rows.astype(jnp.bfloat16)
 
-        pack(top, bottom, keep)
         for half in range(2):
-            for index in range(len(PARTS)):
-                for k in range(3):
-                    send_fresh(lead_slot, half, k, index).start()
+            bottom = next(panels) if half else None
+            pack(top, bottom, keep, (half,))
+            for k in range(3):
+                send_fresh(lead_slot, half, k).start()
 
     loads[3].wait()
     for slot in range(2):
         @pl.when(role[slot] != 0)
         def _():
-            for index in range(len(PARTS)):
-                for half in range(2):
-                    send_fresh(slot, half, 0, index).wait_recv()
-        unpack(fresh.at[slot], roots.at[slot])
+            for half in range(2):
+                send_fresh(slot, half, 0).wait_recv()
+        unpack(fresh.at[slot], roots.at[4 + slot])
 
     pre_sq = jnp.zeros((1, 1), jnp.float32)
     unscaled = []
     for b in range(2):
         left, right = (
-            jnp.where(items[0] == k, roots[0], jnp.where(items[1] == k, roots[1], old[k])) for k in (2 * b, 2 * b + 1))
+            roots[jnp.where(items[0] == k, 4, jnp.where(items[1] == k, 5, k))] for k in (2 * b, 2 * b + 1))
         done = jnp.dot(left, own[0, b], preferred_element_type=jnp.float32).astype(jnp.bfloat16)
         unscaled.append(jnp.dot(done, right, preferred_element_type=jnp.float32))
         pre_sq += total_square(unscaled[b])
@@ -268,9 +267,10 @@
             send_across(index).wait_send()
             for k in range(2):
                 send_far(k, index).wait_send()
-            for half in range(2):
-                for k in range(3):
-                    send_fresh(lead_slot, half, k, index).wait_send()
+            if index == 0:
+                for half in range(2):
+                    for k in range(3):
+                        send_fresh(lead_slot, half, k).wait_send()
 
 
 def pinned(array):
@@ -289,7 +289,6 @@
             pltpu.SMEM((1, 4), jnp.int32),
             pltpu.SMEM((1,), jnp.int32),
             pltpu.VMEM((1, 2, N, N), bf16),
-            pltpu.VMEM((4, N, N), bf16),
             pltpu.VMEM((2, 2, HALF, T), f32),
             pltpu.VMEM((2, 2, HALF, T), bf16),
             pltpu.VMEM((7, HALF, T), bf16),
@@ -299,13 +298,13 @@
             pltpu.VMEM((2, HALF, T), f32),
             pltpu.VMEM((2, 2, HALF, T), bf16),
             pltpu.VMEM((N, N), f32),
-            pltpu.VMEM((2, N, N), bf16),
+            pltpu.VMEM((6, N, N), bf16),
             pltpu.VMEM((PEERS, 8, T), f32),
             dma, dma, dma, dma,
             dma((2, 2, parts)), dma((7, parts)),
             dma((2, parts)), dma((2, parts)),
             dma((parts,)), dma((parts,)),
-            dma((2, 3, parts)), dma((2, 2, parts)),
+            dma((2, 3)), dma((2, 2)),
             dma((PEERS,)), dma((PEERS,)),
             pltpu.SemaphoreType.REGULAR, pltpu.SemaphoreType.REGULAR,
         ],

time: 59.6 us -> 58.7 us (0.985)
  Pallas kernels: 57.8 us -> 57 us
    pallas_call x1, Pallas kernels: 57.8 us -> 57 us  [body(): pl.pallas_call(kernel, out_shape=jax.ShapeDtypeStruct((1, 2, N, N), bf16)...]
where the time goes in v6:
time: 58.7 us; the launch traced here: 58.6 us
  Pallas kernels  57 us (97%)
  local copies, waits for them, and re-layouts  0.97 us (2%)
  between operations  0.66 us (1%)
    pallas_call x1, Pallas kernels, body(): pl.pallas_call(kernel, out_shape=jax.ShapeDtypeStruct((1, 2, N, N), bf16)...  57 us

profile of v6, /device:TPU:1, one launch (start us, length us, event | category | flops | bytes accessed | tf_op | source)
XLA Modules:
  0.0 58.6 jit_solution(2883540446642115929)
XLA Ops:
  0.7 57.0 %refresh.1 = bf16[1,2,512,512]{3,2,1,0:T(8,128)(2,1)S(1)} custom-call(s32[1,4]{1,0:T(1,128)} %order.1, s32[1]{0:T(128)S(6)} %copy.6.offset, bf16[1,2,512,512]{3,2,1,0:T(8,128)(2,1)} %grads.1, bf16[4,512,512]{2,1,0:T(8,128)(2,1)} %prev.1), custom_call_target="tpu_custom_call" | custom-call | flops 2684354560 | bytes 4194304 | tf_op jit(solution)/shard_map/refresh/pallas_call | solution.py:283
  57.7 1.0 %copy.7 = bf16[1,2,512,512]{3,2,1,0:T(8,128)(2,1)} copy(bf16[1,2,512,512]{3,2,1,0:T(8,128)(2,1)S(1)} %refresh.1) | data formatting | bytes 2097152

commit v7 on v6

--- a/solution.py
+++ b/solution.py
@@ -97,7 +97,7 @@
 
     loads = [pltpu.make_async_copy(*refs) for refs in (
         (order, order_here, order_sem), (offset, offset_here, offset_sem), (grads, own, own_sem), (prev, roots.at[pl.ds(0, 4)], old_sem))]
-    for load in loads:
+    for load in loads[:3]:
         load.start()
 
     def along(step, flip=False):
@@ -148,6 +148,7 @@
     loads[1].wait()
     items = [order_here[0, (offset_here[0] + slot) % 4] for slot in range(2)]
     loads[2].wait()
+    loads[3].start()
     for slot in range(2):
         item = items[slot]
         picked = own[0, item // 2]
@@ -212,7 +213,7 @@
         for half in range(2):
             bottom = next(panels) if half else None
             pack(top, bottom, keep, (half,))
-            for k in range(3):
+            for k in (1, 2, 0):
                 send_fresh(lead_slot, half, k).start()
 
     loads[3].wait()

time: 58.7 us -> 58.2 us (level); the launches traced: 58.6 us -> 57.2 us
  Pallas kernels: 57 us -> 55.5 us
    pallas_call x1, Pallas kernels: 57 us -> 55.5 us  [body(): pl.pallas_call(kernel, out_shape=jax.ShapeDtypeStruct((1, 2, N, N), bf16)...]
where the time goes in v7:
time: 58.2 us; the launch traced here: 57.2 us
  Pallas kernels  55.5 us (95%)
  local copies, waits for them, and re-layouts  0.97 us (2%)
  between operations  0.66 us (1%)
    pallas_call x1, Pallas kernels, body(): pl.pallas_call(kernel, out_shape=jax.ShapeDtypeStruct((1, 2, N, N), bf16)...  55.5 us

profile of v7, /device:TPU:1, one launch (start us, length us, event | category | flops | bytes accessed | tf_op | source)
XLA Modules:
  0.0 57.2 jit_solution(6849653653781826351)
XLA Ops:
  0.7 55.5 %refresh.1 = bf16[1,2,512,512]{3,2,1,0:T(8,128)(2,1)S(1)} custom-call(s32[1,4]{1,0:T(1,128)} %order.1, s32[1]{0:T(128)S(6)} %copy.6.offset, bf16[1,2,512,512]{3,2,1,0:T(8,128)(2,1)} %grads.1, bf16[4,512,512]{2,1,0:T(8,128)(2,1)} %prev.1), custom_call_target="tpu_custom_call" | custom-call | flops 2684354560 | bytes 4194304 | tf_op jit(solution)/shard_map/refresh/pallas_call | solution.py:284
  56.2 1.0 %copy.7 = bf16[1,2,512,512]{3,2,1,0:T(8,128)(2,1)} copy(bf16[1,2,512,512]{3,2,1,0:T(8,128)(2,1)S(1)} %refresh.1) | data formatting | bytes 2097152

commit v8 on v7

--- a/solution.py
+++ b/solution.py
@@ -69,7 +69,7 @@
 def next_state(a, square=None):
     e2 = ((small(a, a) if square is None else square) - 10.0 * a) * 0.0625
     e4 = 3.125 * e2 + small(e2, e2)
-    return 2.44140625 * a + small(e4, a)
+    return lambda rows: 2.44140625 * a[rows] + small(e4[rows], a)
 
 
 def inverse_root(stat):
@@ -79,13 +79,14 @@
     square = small(ridged, ridged)
     start = 2.5 / jnp.sqrt(total_square(ridged))
     a = start * ridged
-    b = next_state(a, (start * start) * square)
-    c = next_state(b)
+    b = next_state(a, (start * start) * square)(slice(0, N))
+    c_rows = next_state(b)
     g = small(a, b) * 0.0625 - 0.3125 * (a + b)
     scale = jnp.sqrt(jnp.sqrt(start))
     for rows, columns in ((slice(0, 256), slice(0, N)), (slice(256, N), slice(256, N))):
-        yield scale * (1.953125 * eye[rows, columns] + 1.25 * g[rows, columns] - 0.390625 * c[rows, columns]
-                       - 0.25 * small(g[rows], c[:, columns]))
+        c = c_rows(rows)
+        yield scale * (1.953125 * eye[rows, columns] + 1.25 * g[rows, columns] - 0.390625 * c[:, columns]
+                       - 0.25 * small(c, g[:, columns]))
 
 
 def kernel(order, offset, grads, prev, out, order_here, offset_here, own, stat, sent, near, mine, far, across, both, fresh,

time: 58.2 us -> 58.2 us (level)
  no operation moved by 1% of the time
where the time goes in v8:
time: 58.2 us; the launch traced here: 57.1 us
  Pallas kernels  55.5 us (95%)
  local copies, waits for them, and re-layouts  0.97 us (2%)
  between operations  0.66 us (1%)
    pallas_call x1, Pallas kernels, body(): pl.pallas_call(kernel, out_shape=jax.ShapeDtypeStruct((1, 2, N, N), bf16)...  55.5 us

profile of v8, /device:TPU:1, one launch (start us, length us, event | category | flops | bytes accessed | tf_op | source)
XLA Modules:
  0.0 57.1 jit_solution(18086188386908890905)
XLA Ops:
  0.7 55.5 %refresh.1 = bf16[1,2,512,512]{3,2,1,0:T(8,128)(2,1)S(1)} custom-call(s32[1,4]{1,0:T(1,128)} %order.1, s32[1]{0:T(128)S(6)} %copy.6.offset, bf16[1,2,512,512]{3,2,1,0:T(8,128)(2,1)} %grads.1, bf16[4,512,512]{2,1,0:T(8,128)(2,1)} %prev.1), custom_call_target="tpu_custom_call" | custom-call | flops 2684354560 | bytes 4194304 | tf_op jit(solution)/shard_map/refresh/pallas_call | solution.py:285
  56.2 1.0 %copy.7 = bf16[1,2,512,512]{3,2,1,0:T(8,128)(2,1)} copy(bf16[1,2,512,512]{3,2,1,0:T(8,128)(2,1)S(1)} %refresh.1) | data formatting | bytes 2097152
